TPU v7x, 32 devices: a whole 2x2x4 slice. The times are simulated.
32 devices in a mesh: pair: 4 (over y, x), grid: 8 (over z, core).
Axes of the slice: x: 2, y: 2, z: 4, core: 2. Of those that a mesh axis runs over, the one named last changes fastest.
Arguments:
- cycle_matrix: bfloat16 [24576, 24576], P('grid', 'pair'), may hold values from -0.0390625 to 0.0390625
- amplitudes: bfloat16 [256, 24576], P(None, ('pair', 'grid')), may hold values from -6 to 6
- fit_panel: bfloat16 [4, 384, 1024], P(None, 'grid', 'pair'), may hold values from -0.1875 to 0.1875
- pair_amps: bfloat16 [1024, 384, 384], P('pair', 'grid'), may hold values from -0.59765625 to 0.59765625
- pair_list: int32 [1024], P('pair'), may hold values from 0 to 4095, as said below
- window_list: int32 [384], replicated, may hold values from 0 to 383, each once
- occ_energy: float32 [64], replicated, may hold values from -2 to -0.5
- vir_energy: float32 [384], replicated, may hold values from 0.5 to 3
Outputs:
- cycle_update: bfloat16 [256, 24576], P('pair', 'grid')
- ladder_update: float32 [1024, 16], P('pair')
Inputs may be any that keep to these rules, and one draw needn't show every extreme that they name: `pair_list`: distinct pair indices i * 64 + j. `window_list`: each virtual orbital once.
All inputs are finite; a program needn't handle non-finite values.
Results may differ from a plain program's by a relative error of at most 0.0031.
Values may be sent and summed in bfloat16 or wider, within the bound.
A program may use at most 128 MiB of HBM per device.

v0:
```python
import jax
import jax.numpy as jnp
from jax import lax
from jax.sharding import PartitionSpec as P

O = 64
V = 384
W = 4


def lookup(table, index):
    hits = index[:, None] == jnp.arange(table.shape[0], dtype=jnp.int32)[None, :]
    return jnp.sum(jnp.where(hits, table[None, :], jnp.float32(0.0)), axis=1)


def local(
    cycle_matrix, amplitudes, fit_panel, pair_amps, pair_list, window_list, occ_energy, vir_energy
):
    window_energy = lookup(vir_energy, window_list[:W])
    local_rows = cycle_matrix.shape[0]
    partial_cycle = lax.dot_general(
        lax.all_gather(amplitudes, "grid", axis=1, tiled=True),
        cycle_matrix,
        (((1,), (1,)), ((), ())),
        preferred_element_type=jnp.float32,
    )
    cycle_sum = lax.psum_scatter(partial_cycle, "pair", scatter_dimension=0, tiled=True)
    column_ids = lax.axis_index("pair") * cycle_sum.shape[0] + jnp.arange(
        cycle_sum.shape[0], dtype=jnp.int32
    )
    row_ids = lax.axis_index("grid") * local_rows + jnp.arange(local_rows, dtype=jnp.int32)
    col_energy = lookup(occ_energy, column_ids // W) - lookup(window_energy, column_ids % W)
    row_energy = lookup(occ_energy, row_ids // V) - lookup(vir_energy, row_ids % V)
    cycle_update = (cycle_sum / (col_energy[:, None] + row_energy[None, :])).astype(jnp.bfloat16)
    full_aux = lax.all_gather(fit_panel, "pair", axis=2, tiled=True)
    tile = jnp.einsum(
        "acq,bdq->abcd",
        full_aux,
        lax.all_gather(full_aux, "grid", axis=1, tiled=True),
        preferred_element_type=jnp.float32,
    ).astype(jnp.bfloat16)
    flat_amps = pair_amps.reshape(pair_amps.shape[0], pair_amps.shape[1] * pair_amps.shape[2])
    flat_tile = tile.reshape(W * W, tile.shape[2] * tile.shape[3])
    partial_ladder = lax.dot_general(
        flat_amps, flat_tile, (((1,), (1,)), ((), ())), preferred_element_type=jnp.float32
    )
    ladder = lax.psum(partial_ladder, "grid")
    pair_energy = lookup(occ_energy, pair_list // O) + lookup(occ_energy, pair_list % O)
    win_pair = (window_energy[:, None] + window_energy[None, :]).reshape(W * W)
    ladder_update = ladder / (pair_energy[:, None] - win_pair[None, :])
    return (cycle_update, ladder_update)


def solution(mesh):
    return jax.shard_map(
        local,
        mesh=mesh,
        in_specs=(
            P("grid", "pair"),
            P(None, ("pair", "grid")),
            P(None, "grid", "pair"),
            P("pair", "grid", None),
            P("pair"),
            P(),
            P(),
            P(),
        ),
        out_specs=(P("pair", "grid"), P("pair", None)),
        check_vma=False,
    )
```

profile of v0, /device:TPU:0, one launch (start us, length us, event | category | flops | bytes accessed | tf_op | source)
XLA Modules:
  0.0 143.8 jit_solution(6767259012352079079)
XLA Ops:
  7.2 0.0 all-gather.3.cloned.1.call-start
  7.2 0.7 all-gather.3.cloned.1.call-update
  7.9 0.0 all-gather.5.cloned.1.call-start
  7.9 15.1 %all_gather.10 = bf16[4,48,1024]{2,1,0:T(8,128)(2,1)} all-gather(bf16[4,48,256]{2,1,0:T(8,128)(2,1)} %param.10), channel_id=1, replica_groups=mesh['pair'=4,'grid'=8] {'pair'}, dimensions={2}, use_global_device_ids=true | all-gather | bytes 491520 | tf_op jit(solution)/shard_map/all_gather | solution.py:35
  23.0 0.0 all-gather.5.cloned.1.call-update
  23.0 0.0 reduce-scatter.2.cloned.1.call-start
  23.1 27.5 %all-gather.3.cloned.1.call-done = bf16[256,6144]{1,0:T(8,128)(2,1)} async-done(((bf16[256,768]{1,0:T(8,128)(2,1)}), bf16[256,6144]{1,0:T(8,128)(2,1)}) %all-gather.3.cloned.1.call-update) | async-done | bytes 3145744 | tf_op jit(solution)/shard_map/all_gather | solution.py:22
  50.6 18.4 %fusion.14 = f32[256,3072]{1,0:T(8,128)} fusion(bf16[256,6144]{1,0:T(8,128)(2,1)} %all-gather.3.cloned.1.call-done, bf16[3072,6144]{1,0:T(8,128)(2,1)} %param.8), kind=kOutput, calls=%fused_computation.45 | convolution fusion | flops 9663676416 | bytes 44040192 | tf_op jit(solution)/shard_map/dot_general | solution.py:21
  69.0 0.0 reduce-scatter.2.cloned.1.call-update
  69.1 0.0 copy-start.1
  69.1 0.0 slice-start
  69.1 0.0 copy-start.3
  69.1 0.0 copy-start.2
  69.1 10.3 %copy.14 = bf16[32,8,48,384]{3,1,2,0:T(8,128)(2,1)} copy(bf16[32,8,48,384]{3,2,1,0:T(8,128)(2,1)} %bitcast.26) | data formatting | bytes 18874368
  79.5 0.0 slice-done
  79.5 0.2 select_reduce_fusion.5
  79.7 0.1 broadcast_add_fusion
  79.7 0.1 add.121
  79.8 0.1 select_reduce_fusion.2
  80.0 0.1 select_reduce_fusion.6
  80.1 0.2 select_reduce_fusion.4
  80.3 0.2 select_reduce_fusion.1
  80.5 2.0 %select_reduce_fusion = f32[3072]{0:T(1024)S(1)} fusion(f32[384]{0:T(512)S(1)} %copy-done.1, s32[3072]{0:T(1024)S(1)} %get-tuple-element.6), kind=kLoop, calls=%fused_computation | loop fusion | flops 3535872 | bytes 26112 | tf_op jit(solution)/shard_map/reduce_sum | solution.py:13
  82.5 6.9 %all-gather.5.cloned.1.call-done = bf16[4,384,1024]{2,1,0:T(8,128)(2,1)} async-done(((bf16[4,48,1024]{2,1,0:T(8,128)(2,1)}), bf16[4,384,1024]{2,1,0:T(8,128)(2,1)}) %all-gather.5.cloned.1.call-update) | async-done | bytes 3145744 | tf_op jit(solution)/shard_map/all_gather | solution.py:39
  89.4 3.1 %fusion.5 = bf16[4,4,48,384]{3,2,0,1:T(8,128)(2,1)S(1)} fusion(bf16[4,384,1024]{2,1,0:T(8,128)(2,1)} %all-gather.5.cloned.1.call-done, bf16[4,48,1024]{2,1,0:T(8,128)(2,1)S(1)} %copy-done), kind=kOutput, calls=%fused_computation.5 | convolution fusion | flops 604274688 | bytes 4128768 | tf_op jit(solution)/shard_map/acq,bdq->abcd/dot_general | solution.py:36
  92.5 0.1 copy.11
  92.6 0.1 copy.13
  92.7 6.2 %convolution_bitcast_fusion = f32[256,16]{0,1:T(8,128)S(1)} fusion(bf16[16,18432]{1,0:T(8,128)(2,1)S(1)} %bitcast.27, bf16[256,18432]{1,0:T(8,128)(2,1)} %bitcast.25), kind=kOutput, calls=%fused_computation.6 | convolution fusion | flops 150994944 | bytes 10043392 | tf_op jit(solution)/shard_map/dot_general | solution.py:44
  98.9 26.9 %psum.7 = f32[256,16]{0,1:T(8,128)S(1)} all-reduce(f32[256,16]{0,1:T(8,128)S(1)} %convolution_bitcast_fusion), channel_id=1, replica_groups=mesh['pair'=4,'grid'=8] {'grid'}, use_global_device_ids=true, to_apply=%region_6.7 | all-reduce | flops 4096 | bytes 32768 | tf_op jit(solution)/shard_map/psum | solution.py:47
  125.8 0.7 subtract_divide_fusion
  126.5 8.7 %reduce-scatter.2.cloned.1.call-done = f32[64,3072]{1,0:T(8,128)} async-done(((f32[256,3072]{1,0:T(8,128)}), f32[64,3072]{1,0:T(8,128)}) %reduce-scatter.2.cloned.1.call-update) | async-done | bytes 786448 | tf_op jit(solution)/shard_map/reduce_scatter | solution.py:27
  135.3 2.1 %divide_convert_fusion = bf16[64,3072]{1,0:T(8,128)(2,1)} fusion(f32[64,3072]{1,0:T(8,128)} %reduce-scatter.2.cloned.1.call-done, f32[3072]{0:T(1024)S(1)} %sub.48, f32[64]{0:T(128)S(1)} %sub.46), kind=kLoop, calls=%fused_computation.7 | loop fusion | flops 589824 | bytes 1192192 | tf_op jit(solution)/shard_map/convert_element_type | solution.py:34
  (11 shorter events, 0.1 us)
Async XLA Ops:
  7.2 43.5 %all-gather.3.cloned.1.call-start = ((), (), s32[]{:S(2)}) async-start(), calls=%async_computation.1 | async-start | bytes 3538944 | tf_op jit(solution)/shard_map/all_gather | solution.py:22
  7.9 81.5 %all-gather.5.cloned.1.call-start = ((), (), s32[]{:S(2)}) async-start(), calls=%async_computation.3 | async-start | bytes 3538944 | tf_op jit(solution)/shard_map/all_gather | solution.py:39
  23.0 112.2 %reduce-scatter.2.cloned.1.call-start = ((), (), s32[]{:S(2)}) async-start(), calls=%async_computation.2 | async-start | bytes 3932160 | tf_op jit(solution)/shard_map/reduce_scatter | solution.py:27
  69.1 10.4 %copy-start.1 = (f32[384]{0:T(512)S(1)}, f32[384]{0:T(512)}, u32[]{:S(2)}) copy-start(f32[384]{0:T(512)} %param.15) | copy-start | bytes 4612
  69.1 10.4 %slice-start = ((s32[384]{0:T(512)}), s32[4]{0:T(128)S(1)}, s32[]{:S(2)}) async-start(s32[384]{0:T(512)} %param.13), calls=%async_computation.4 | async-start | bytes 1024 | tf_op jit(solution)/shard_map/slice | solution.py:19
  69.1 10.7 %copy-start.3 = (s32[256]{0:T(256)S(1)}, s32[256]{0:T(256)}, u32[]{:S(2)}) copy-start(s32[256]{0:T(256)} %param.12) | copy-start | bytes 3076
  69.1 10.7 %copy-start.2 = (f32[64]{0:T(128)S(1)}, f32[64]{0:T(128)}, u32[]{:S(2)}) copy-start(f32[64]{0:T(128)} %param.14) | copy-start | bytes 772
  69.1 20.3 %copy-start = (bf16[4,48,1024]{2,1,0:T(8,128)(2,1)S(1)}, bf16[4,48,1024]{2,1,0:T(8,128)(2,1)}, u32[]{:S(2)}) copy-start(bf16[4,48,1024]{2,1,0:T(8,128)(2,1)} %all_gather.10) | copy-start | bytes 1179652
Sparse Core Ops, SparseCore 0:
  9.6 40.9 all-gather.2
  52.2 37.1 all-gather.4
  92.4 42.8 reduce-scatter.1
where the time goes:
time: 144 us
  waiting for transfers between devices  43.9 us (30%)
  blocking collectives  42 us (29%)
  matrix products  27.7 us (19%)
  between operations  13.9 us (10%)
  local copies, waits for them, and re-layouts  10.6 us (7%)
  other arithmetic  5.64 us (4%)
    all_gather x1, waiting for transfers between devices, local(): lax.all_gather(amplitudes, 'grid', axis=1, tiled=True)  27.5 us
    psum x1, blocking collectives, local(): ladder = lax.psum(partial_ladder, 'grid')  26.9 us
    dot_general x1, matrix products, local(): lax.dot_general(lax.all_gather(amplitudes, 'grid', axis=1, tiled=True), c...  18.4 us
    all_gather x1, blocking collectives, local(): full_aux = lax.all_gather(fit_panel, 'pair', axis=2, tiled=True)  15.1 us
    unnamed x10, local copies, waits for them, and re-layouts  10.5 us
    reduce_scatter x1, waiting for transfers between devices, local(): lax.psum_scatter(partial_cycle, 'pair', scatter_dimension=0, tiled=True)  8.72 us
    all_gather x1, waiting for transfers between devices, local(): lax.all_gather(full_aux, 'grid', axis=1, tiled=True)  6.88 us
    dot_general x1, matrix products, local(): lax.dot_general(flat_amps, flat_tile, (((1,), (1,)), ((), ())), preferred...  6.21 us
  transfers between devices with their start and end apart: 3, of which 3 were waited for; matrix products, arithmetic and copies ran while one was open for 29% of the time, Pallas kernels for 0%

commit v1 on v0

v1 whole, which is shorter than its diff:
```python
import functools

import jax
import jax.numpy as jnp
from jax import lax
from jax.experimental import pallas as pl
from jax.experimental.pallas import tpu as pltpu
from jax.sharding import PartitionSpec as P

O = 64
V = 384
W = 4
CHUNKS = 4
SUB = 16
MESH = pl.DeviceIdType.MESH
NT = (((1,), (1,)), ((), ()))


def lookup(table, index):
    hits = index[:, None] == jnp.arange(table.shape[0], dtype=jnp.int32)[None, :]
    return jnp.sum(jnp.where(hits, table[None, :], jnp.float32(0.0)), axis=1)


def dot_nt(a, b):
    return lax.dot_general(a, b, NT, preferred_element_type=jnp.float32)


def kernel(
    n_p, n_g, amps, mat, fit, pairs, cyc_out, lad_out,
    abuf, mbuf, tbuf, xbuf, ybuf, zbuf, wt, sbuf, lbuf, acc, rsend, rrecv,
    msem, lsem, arecv, asend, xrecv, xsend, zrecv, zsend, rrsem, rssem, lrecv, lsend,
):
    n_z = n_g // 2
    p = lax.axis_index("pair")
    g = lax.axis_index("grid")
    z = g // 2
    c = g % 2
    sib = z * 2 + 1 - c
    rows = abuf.shape[2]
    depth = abuf.shape[3]
    h = rows // CHUNKS
    cols = mbuf.shape[1]
    own_c = ybuf.shape[2]
    n_pairs = tbuf.shape[0]
    item_y = CHUNKS
    tile_n = 512 if cols % 512 == 0 else cols
    q_of = [lax.rem(p + k, n_p) for k in range(1, n_p)]
    g_of = [lax.rem(g + k, n_g) for k in range(1, n_g)]

    load_x = pltpu.make_async_copy(fit, xbuf.at[p], lsem.at[0])
    load_x.start()
    load_a = pltpu.make_async_copy(amps, abuf.at[g], lsem.at[1])
    load_a.start()

    def load_m(s):
        at = pl.multiple_of(s * depth, 128)
        return pltpu.make_async_copy(mat.at[:, pl.ds(at, depth)], mbuf.at[s], msem.at[s])

    load_m(g).start()
    load_m(sib).start()
    for t in range(1, n_z):
        for d in (1, -1):
            sz = z - d * t

            @pl.when(jnp.logical_and(sz >= 0, sz < n_z))
            def _():
                load_m(sz * 2 + c).start()
                load_m(sz * 2 + 1 - c).start()
    load_t = pltpu.make_async_copy(pairs, tbuf, lsem.at[2])
    load_t.start()

    barrier = pltpu.get_barrier_semaphore()
    for q in q_of:
        pl.semaphore_signal(barrier, inc=1, device_id={"pair": q}, device_id_type=MESH)
    for q in g_of:
        pl.semaphore_signal(barrier, inc=1, device_id={"grid": q}, device_id_type=MESH)
    pl.semaphore_wait(barrier, n_p - 1 + n_g - 1)

    def shard(item, s):
        if item == item_y:
            return ybuf.at[:, s]
        return abuf.at[s, :, pl.ds(item * h, h), :]

    def hop(item, s, kind, target):
        ref = shard(item, s)
        return pltpu.make_async_remote_copy(
            src_ref=ref, dst_ref=ref, send_sem=asend.at[item, s, kind], recv_sem=arecv.at[item, s],
            device_id={"grid": target}, device_id_type=MESH,
        )

    def own_send(item, act):
        @pl.when(z + 1 < n_z)
        def _():
            act(hop(item, g, 0, g + 2))

        @pl.when(z >= 1)
        def _():
            act(hop(item, g, 2, g - 2))

        act(hop(item, g, 1, sib))

    def each_line(t, body):
        for d in (1, -1):
            sz = z - d * t

            @pl.when(jnp.logical_and(sz >= 0, sz < n_z))
            def _():
                body(d, sz)

    def forward(item, t, wait_first, act):
        def body(d, sz):
            s = sz * 2 + c
            if wait_first:
                hop(item, s, 0, sib).wait_recv()
            nz = z + d

            @pl.when(jnp.logical_and(nz >= 0, nz < n_z))
            def _():
                act(hop(item, s, 0, nz * 2 + c))

            act(hop(item, s, 1, sib))

        each_line(t, body)

    def begin(cp):
        cp.start()

    def product(r, s, first=False):
        if r == 0:
            load_m(s).wait()

        def tile(i, carry):
            at = pl.ds(pl.multiple_of(i * tile_n, 128), tile_n)
            lhs = abuf[s, :, r * h:(r + 1) * h, :].reshape(n_p * h, depth)
            out = dot_nt(lhs, mbuf[s, at, :]).reshape(n_p, h, tile_n)
            if first:
                acc[r, :, :, at] = out
            else:
                acc[r, :, :, at] += out
            return carry

        lax.fori_loop(0, cols // tile_n, tile, 0)

    def scatter(r, k):
        q = q_of[k]
        return pltpu.make_async_remote_copy(
            src_ref=rsend.at[r, q], dst_ref=rrecv.at[p, r], send_sem=rssem.at[r, k],
            recv_sem=rrsem.at[r, p], device_id={"pair": q}, device_id_type=MESH,
        )

    def scatter_wait(r, q):
        pltpu.make_async_remote_copy(
            src_ref=rsend.at[r, q], dst_ref=rrecv.at[q, r], send_sem=rssem.at[r, 0],
            recv_sem=rrsem.at[r, q], device_id={"pair": q}, device_id_type=MESH,
        ).wait_recv()

    def reduce_start(r):
        rsend[r] = acc[r].astype(rsend.dtype)
        for k in range(n_p - 1):
            scatter(r, k).start()

    def reduce_end(r):
        total = acc[r, p]
        for q in q_of:
            scatter_wait(r, q)
            total = total + rrecv[q, r].astype(jnp.float32)
        cyc_out[r * h:(r + 1) * h, :] = total

    def spread(buf, slot, send, recv, k):
        q = q_of[k]
        return pltpu.make_async_remote_copy(
            src_ref=buf.at[slot], dst_ref=buf.at[slot], send_sem=send.at[k], recv_sem=recv.at[slot],
            device_id={"pair": q}, device_id_type=MESH,
        )

    def spread_all(buf, send, recv):
        for k in range(n_p - 1):
            spread(buf, p, send, recv, k).start()

    def spread_wait(buf, send, recv):
        for k in range(n_p - 1):
            spread(buf, q_of[k], send, recv, k).wait_recv()

    def tile_part():
        total = None
        for q in range(n_p):
            term = dot_nt(xbuf[q], ybuf[q].reshape(n_g * own_c, ybuf.shape[3]))
            total = term if total is None else total + term
        zbuf[p] = total.astype(zbuf.dtype)

    def weights():
        for j in range(own_c // SUB):
            for a in range(W):
                for b in range(W):
                    at = (a * W + b) * SUB
                    wt[j, at:at + SUB, :] = zbuf[b, a * own_c + j * SUB:a * own_c + (j + 1) * SUB, :]

    piece = n_pairs // n_z

    def ladder_piece(i):
        at = pl.ds(pl.multiple_of(i * piece, 8), piece)
        total = None
        for j in range(own_c // SUB):
            lhs = tbuf[at, j * SUB:(j + 1) * SUB, :].reshape(piece * SUB, tbuf.shape[2])
            term = dot_nt(lhs, wt[j])
            total = term if total is None else total + term
        total = total.reshape(piece, SUB, W * W * SUB)
        r_id = lax.broadcasted_iota(jnp.int32, (1, SUB, W * W * SUB), 1)
        c_id = lax.broadcasted_iota(jnp.int32, (1, SUB, W * W * SUB), 2)
        sbuf[at, :] = jnp.sum(jnp.where(r_id == c_id % SUB, total, 0.0), axis=1)

    def lad_copy(k, slot):
        return pltpu.make_async_remote_copy(
            src_ref=lbuf.at[slot], dst_ref=lbuf.at[slot], send_sem=lsend.at[k], recv_sem=lrecv.at[slot],
            device_id={"grid": g_of[k]}, device_id_type=MESH,
        )

    def ladder_send():
        row = lax.broadcasted_iota(jnp.int32, (W * W, W * W * SUB), 0)
        col = lax.broadcasted_iota(jnp.int32, (W * W, W * W * SUB), 1)
        ones = jnp.where(row == col // SUB, 1.0, 0.0).astype(jnp.float32)
        lbuf[g] = lax.dot_general(
            ones, sbuf[...], NT, precision=lax.Precision.HIGHEST, preferred_element_type=jnp.float32
        )
        for k in range(n_g - 1):
            lad_copy(k, g).start()

    def ladder_end():
        for k in range(n_g - 1):
            lad_copy(k, g_of[k]).wait_recv()
        total = lbuf[0]
        for s in range(1, n_g):
            total = total + lbuf[s]
        lad_out[...] = total

    def chunk(r, extra):
        if r + 1 < CHUNKS:
            own_send(r + 1, begin)
        product(r, g, first=True)
        if r == 0:
            spread_wait(xbuf, xsend, xrecv)
            mine = pl.ds(pl.multiple_of(p * own_c, SUB), own_c)
            ybuf[:, g] = xbuf[:, mine, :]
            own_send(item_y, begin)
        hop(r, sib, 1, sib).wait_recv()
        product(r, sib)

        def step(t, carry):
            forward(r, t, True, begin)
            if r == 0:
                forward(item_y, t, True, begin)
            if extra is not None:
                extra(t)

            def use(d, sz):
                product(r, sz * 2 + c)
                s = sz * 2 + 1 - c
                hop(r, s, 1, sib).wait_recv()
                product(r, s)

            each_line(t, use)
            return carry

        lax.fori_loop(1, n_z, step, 0)
        reduce_start(r)

    load_x.wait()
    spread_all(xbuf, xsend, xrecv)
    load_a.wait()
    own_send(0, begin)
    chunk(0, None)
    hop(item_y, sib, 1, sib).wait_recv()

    def rest(t, carry):
        each_line(t, lambda d, sz: hop(item_y, sz * 2 + 1 - c, 1, sib).wait_recv())
        return carry

    lax.fori_loop(1, n_z, rest, 0)
    tile_part()
    spread_all(zbuf, zsend, zrecv)
    chunk(1, None)
    reduce_end(0)
    spread_wait(zbuf, zsend, zrecv)
    weights()
    load_t.wait()
    for r in range(2, CHUNKS):
        if r == 2:
            chunk(r, ladder_piece)
            ladder_piece(0)
            ladder_send()
        else:
            chunk(r, None)
        if r + 1 < CHUNKS:
            reduce_end(r - 1)
    ladder_end()
    reduce_end(CHUNKS - 2)
    reduce_end(CHUNKS - 1)

    def sent(cp):
        cp.wait_send()

    for item in range(CHUNKS + 1):
        own_send(item, sent)

        def step(t, carry, item=item):
            forward(item, t, False, sent)
            return carry

        lax.fori_loop(1, n_z, step, 0)
    for k in range(n_p - 1):
        spread(xbuf, p, xsend, xrecv, k).wait_send()
        spread(zbuf, p, zsend, zrecv, k).wait_send()
        for r in range(CHUNKS):
            scatter(r, k).wait_send()
    for k in range(n_g - 1):
        lad_copy(k, g).wait_send()


def fused(n_p, n_g, amplitudes, cycle_matrix, fit_panel, pair_amps):
    rows = amplitudes.shape[0] // n_p
    depth = amplitudes.shape[1]
    cols = cycle_matrix.shape[0]
    n_pairs, own_c, n_v = pair_amps.shape
    aux = fit_panel.shape[2]
    h = rows // CHUNKS
    bf, f32 = jnp.bfloat16, jnp.float32
    dma = pltpu.SemaphoreType.DMA
    hbm = pl.BlockSpec(memory_space=pl.ANY)
    vmem = pl.BlockSpec(memory_space=pltpu.VMEM)
    return pl.pallas_call(
        functools.partial(kernel, n_p, n_g),
        out_shape=(
            jax.ShapeDtypeStruct((rows, cols), f32),
            jax.ShapeDtypeStruct((W * W, n_pairs), f32),
        ),
        in_specs=[hbm] * 4,
        out_specs=(vmem, vmem),
        scratch_shapes=[
            pltpu.VMEM((n_g, n_p, rows, depth), bf),
            pltpu.VMEM((n_g, cols, depth), bf),
            pltpu.VMEM((n_pairs, own_c, n_v), bf),
            pltpu.VMEM((n_p, W * own_c, aux), bf),
            pltpu.VMEM((n_p, n_g, own_c, aux), bf),
            pltpu.VMEM((n_p, W * own_c, n_v), bf),
            pltpu.VMEM((own_c // SUB, W * W * SUB, n_v), bf),
            pltpu.VMEM((n_pairs, W * W * SUB), f32),
            pltpu.VMEM((n_g, W * W, n_pairs), f32),
            pltpu.VMEM((CHUNKS, n_p, h, cols), f32),
            pltpu.VMEM((CHUNKS, n_p, h, cols), bf),
            pltpu.VMEM((n_p, CHUNKS, h, cols), bf),
            dma((n_g,)),
            dma((3,)),
            dma((CHUNKS + 1, n_g)),
            dma((CHUNKS + 1, n_g, 3)),
            dma((n_p,)),
            dma((n_p,)),
            dma((n_p,)),
            dma((n_p,)),
            dma((CHUNKS, n_p)),
            dma((CHUNKS, n_p)),
            dma((n_g,)),
            dma((n_g,)),
        ],
        compiler_params=pltpu.CompilerParams(
            collective_id=0, has_side_effects=True, vmem_limit_bytes=63 * 1024 * 1024
        ),
    )(
        amplitudes.reshape(n_p, rows, depth),
        cycle_matrix,
        fit_panel.reshape(W * own_c, aux),
        pair_amps,
    )


def plain(n_p, n_g, amplitudes, cycle_matrix, fit_panel, pair_amps):
    partial_cycle = lax.dot_general(
        lax.all_gather(amplitudes, "grid", axis=1, tiled=True),
        cycle_matrix,
        NT,
        preferred_element_type=jnp.float32,
    )
    cycle_sum = lax.psum_scatter(partial_cycle, "pair", scatter_dimension=0, tiled=True)
    full_aux = lax.all_gather(fit_panel, "pair", axis=2, tiled=True)
    tile = jnp.einsum(
        "acq,bdq->abcd",
        full_aux,
        lax.all_gather(full_aux, "grid", axis=1, tiled=True),
        preferred_element_type=jnp.float32,
    ).astype(jnp.bfloat16)
    flat_amps = pair_amps.reshape(pair_amps.shape[0], pair_amps.shape[1] * pair_amps.shape[2])
    flat_tile = tile.reshape(W * W, tile.shape[2] * tile.shape[3])
    partial_ladder = lax.dot_general(
        flat_amps, flat_tile, NT, preferred_element_type=jnp.float32
    )
    return cycle_sum, lax.psum(partial_ladder, "grid").T


def suits(n_p, n_g, amplitudes, fit_panel, pair_amps):
    rows = amplitudes.shape[0] // n_p
    return (
        n_p == W
        and n_g % 2 == 0
        and rows % (CHUNKS * SUB) == 0
        and amplitudes.shape[1] % 128 == 0
        and fit_panel.shape[2] % 128 == 0
        and pair_amps.shape[1] % SUB == 0
        and pair_amps.shape[2] % 128 == 0
        and pair_amps.shape[0] % (8 * (n_g // 2)) == 0
    )


def local(
    n_p, n_g,
    cycle_matrix, amplitudes, fit_panel, pair_amps, pair_list, window_list, occ_energy, vir_energy
):
    window_energy = lookup(vir_energy, window_list[:W])
    local_rows = cycle_matrix.shape[0]
    form = fused if suits(n_p, n_g, amplitudes, fit_panel, pair_amps) else plain
    cycle_sum, ladder = form(n_p, n_g, amplitudes, cycle_matrix, fit_panel, pair_amps)
    column_ids = lax.axis_index("pair") * cycle_sum.shape[0] + jnp.arange(
        cycle_sum.shape[0], dtype=jnp.int32
    )
    row_ids = lax.axis_index("grid") * local_rows + jnp.arange(local_rows, dtype=jnp.int32)
    col_energy = lookup(occ_energy, column_ids // W) - lookup(window_energy, column_ids % W)
    row_energy = lookup(occ_energy, row_ids // V) - lookup(vir_energy, row_ids % V)
    cycle_update = (cycle_sum / (col_energy[:, None] + row_energy[None, :])).astype(jnp.bfloat16)
    pair_energy = lookup(occ_energy, pair_list // O) + lookup(occ_energy, pair_list % O)
    win_pair = (window_energy[:, None] + window_energy[None, :]).reshape(W * W)
    ladder_update = ladder.T / (pair_energy[:, None] - win_pair[None, :])
    return (cycle_update, ladder_update)


def solution(mesh):
    return jax.shard_map(
        functools.partial(local, mesh.shape["pair"], mesh.shape["grid"]),
        mesh=mesh,
        in_specs=(
            P("grid", "pair"),
            P(None, ("pair", "grid")),
            P(None, "grid", "pair"),
            P("pair", "grid", None),
            P("pair"),
            P(),
            P(),
            P(),
        ),
        out_specs=(P("pair", "grid"), P("pair", None)),
        check_vma=False,
    )
```

time: 144 us -> 121 us (0.84)
  Pallas kernels: 0 us -> 110 us
  waiting for transfers between devices: 43.9 us -> 0 us
  blocking collectives: 42 us -> 0 us
  matrix products: 27.7 us -> 0 us
  between operations: 13.9 us -> 0.72 us
  local copies, waits for them, and re-layouts: 10.6 us -> 0.78 us
  other arithmetic: 5.64 us -> 9.02 us
    pallas_call x0 -> x1, Pallas kernels: none -> 110 us  [fused(): pl.pallas_call(functools.partial(kernel, n_p, n_g), out_shape=(jax.ShapeD...]
    all_gather x2 -> x0, waiting for transfers between devices: 34.4 us -> none  [the longest x1 27.5 us: local(): lax.all_gather(amplitudes, 'grid', axis=1, tiled=True)]
    dot_general x3 -> x0, matrix products: 27.7 us -> none  [the longest x1 18.4 us: local(): lax.dot_general(lax.all_gather(amplitudes, 'grid', axis=1, tiled=True), c...]
    psum x1 -> x0, blocking collectives: 26.9 us -> none  [local(): ladder = lax.psum(partial_ladder, 'grid')]
    all_gather x1 -> x0, blocking collectives: 15.1 us -> none  [local(): full_aux = lax.all_gather(fit_panel, 'pair', axis=2, tiled=True)]
    unnamed x10 -> x4, local copies, waits for them, and re-layouts: 10.5 us -> 0.01 us
    reduce_scatter x1 -> x0, waiting for transfers between devices: 8.72 us -> none  [local(): lax.psum_scatter(partial_cycle, 'pair', scatter_dimension=0, tiled=True)]
    reduce_sum x6, other arithmetic: 2.77 us -> 5.44 us  [lookup(): return jnp.sum(jnp.where(hits, table[None, :], jnp.float32(0.0)), axis=1)]
  transfers between devices with their start and end apart: 3 -> 0, of which waited for: 3 -> 0; matrix products, arithmetic and copies ran while one was open for 29% -> 0% of each run, Pallas kernels for 0% -> 0%
where the time goes in v1:
time: 121 us; the launch traced here: 120 us
  Pallas kernels  110 us (91%)
  other arithmetic  9.02 us (7%)
    pallas_call x1, Pallas kernels, fused(): pl.pallas_call(functools.partial(kernel, n_p, n_g), out_shape=(jax.ShapeD...  110 us
    reduce_sum x6, other arithmetic, lookup(): return jnp.sum(jnp.where(hits, table[None, :], jnp.float32(0.0)), axis=1)  5.44 us

profile of v1, /device:TPU:0, one launch (start us, length us, event | category | flops | bytes accessed | tf_op | source)
XLA Modules:
  0.0 120.3 jit_solution(3855733312235530432)
XLA Ops:
  0.7 0.7 slice.3
  1.3 0.9 select_reduce_fusion.5
  2.2 0.1 select_reduce_fusion.6
  2.3 0.8 select_reduce_fusion.4
  3.2 2.7 %select_reduce_fusion = f32[3072]{0:T(1024)S(1)} fusion(f32[384]{0:T(512)} %param.15, s32[3072]{0:T(1024)S(1)} %get-tuple-element.10), kind=kLoop, calls=%fused_computation | loop fusion | flops 3535872 | bytes 26112 | tf_op jit(solution)/shard_map/reduce_sum | solution.py:21
  5.9 0.8 select_reduce_fusion.1
  6.7 0.0 copy-start.1
  6.8 0.0 copy-start
  6.8 109.8 %shard_map.95 = (f32[64,3072]{1,0:T(8,128)}, f32[16,256]{1,0:T(8,128)}) custom-call(bf16[4,64,768]{2,1,0:T(8,128)(2,1)} %bitcast.4, bf16[3072,6144]{1,0:T(8,128)(2,1)} %mat.1, bf16[192,256]{1,0:T(8,128)(2,1)} %bitcast.5, bf16[256,48,384]{2,1,0:T(8,128)(2,1)} %pairs.1), custom_call_target="tpu_custom_call" | custom-call | tf_op jit(solution)/shard_map/pallas_call | solution.py:330
  116.5 2.1 %divide_convert_fusion = bf16[64,3072]{1,0:T(8,128)(2,1)} fusion(f32[64,3072]{1,0:T(8,128)} %get-tuple-element.4, f32[3072]{0:T(1024)S(1)} %sub.48, f32[64]{0:T(128)S(1)} %sub.46), kind=kLoop, calls=%fused_computation.2 | loop fusion | flops 589824 | bytes 1192192 | tf_op jit(solution)/shard_map/convert_element_type | solution.py:426
  118.6 0.0 copy-done.1
  118.6 0.0 copy-done
  118.6 0.1 select_reduce_fusion.2
  118.7 0.1 broadcast_add_fusion
  118.8 0.1 add.117
  118.9 1.4 %bitcast_divide_fusion = f32[256,16]{0,1:T(8,128)} fusion(f32[16,256]{1,0:T(8,128)} %get-tuple-element.5, f32[16]{0:T(128)S(1)} %add.117, f32[256]{0:T(256)S(1)} %add.113), kind=kLoop, calls=%fused_computation.13 | loop fusion | flops 8192 | bytes 33856 | tf_op jit(solution)/shard_map/div | solution.py:429
  (6 shorter events, 0.1 us)
Async XLA Ops:
  6.7 111.9 %copy-start.1 = (s32[256]{0:T(256)S(1)}, s32[256]{0:T(256)}, u32[]{:S(2)}) copy-start(s32[256]{0:T(256)} %param.12) | copy-start | bytes 3076
  6.8 111.9 %copy-start = (f32[64]{0:T(128)S(1)}, f32[64]{0:T(128)}, u32[]{:S(2)}) copy-start(f32[64]{0:T(128)} %param.14) | copy-start | bytes 772

commit v2 on v1

--- a/solution.py
+++ b/solution.py
@@ -10,7 +10,7 @@
 O = 64
 V = 384
 W = 4
-CHUNKS = 4
+CHUNKS = 2
 SUB = 16
 MESH = pl.DeviceIdType.MESH
 NT = (((1,), (1,)), ((), ()))
@@ -26,8 +26,8 @@
 
 
 def kernel(
-    n_p, n_g, amps, mat, fit, pairs, cyc_out, lad_out,
-    abuf, mbuf, tbuf, xbuf, ybuf, zbuf, wt, sbuf, lbuf, acc, rsend, rrecv,
+    n_p, n_g, amps, mat, fit, pairs, plist, wlist, occ, vir, cyc_out, lad_out,
+    abuf, mbuf, tbuf, xbuf, ybuf, zbuf, wt, sbuf, lbuf, acc, part, rsend, rrecv, cden, rden, lden,
     msem, lsem, arecv, asend, xrecv, xsend, zrecv, zsend, rrsem, rssem, lrecv, lsend,
 ):
     n_z = n_g // 2
@@ -43,7 +43,8 @@
     own_c = ybuf.shape[2]
     n_pairs = tbuf.shape[0]
     item_y = CHUNKS
-    tile_n = 512 if cols % 512 == 0 else cols
+    tile_n = tile_of(cols)
+    tiles = cols // tile_n
     q_of = [lax.rem(p + k, n_p) for k in range(1, n_p)]
     g_of = [lax.rem(g + k, n_g) for k in range(1, n_g)]
 
@@ -131,40 +132,70 @@
 
         def tile(i, carry):
             at = pl.ds(pl.multiple_of(i * tile_n, 128), tile_n)
-            lhs = abuf[s, :, r * h:(r + 1) * h, :].reshape(n_p * h, depth)
-            out = dot_nt(lhs, mbuf[s, at, :]).reshape(n_p, h, tile_n)
+            rhs = abuf[s, :, r * h:(r + 1) * h, :].reshape(n_p * h, depth)
+            out = dot_nt(mbuf[s, at, :], rhs)
             if first:
-                acc[r, :, :, at] = out
+                acc[at, :] = out
             else:
-                acc[r, :, :, at] += out
+                acc[at, :] += out
             return carry
 
-        lax.fori_loop(0, cols // tile_n, tile, 0)
-
-    def scatter(r, k):
-        q = q_of[k]
+        lax.fori_loop(0, tiles, tile, 0)
+
+    def scatter(r, i, k, q, slot):
+        at = slice(i * tile_n, (i + 1) * tile_n)
         return pltpu.make_async_remote_copy(
-            src_ref=rsend.at[r, q], dst_ref=rrecv.at[p, r], send_sem=rssem.at[r, k],
-            recv_sem=rrsem.at[r, p], device_id={"pair": q}, device_id_type=MESH,
-        )
-
-    def scatter_wait(r, q):
-        pltpu.make_async_remote_copy(
-            src_ref=rsend.at[r, q], dst_ref=rrecv.at[q, r], send_sem=rssem.at[r, 0],
-            recv_sem=rrsem.at[r, q], device_id={"pair": q}, device_id_type=MESH,
-        ).wait_recv()
+            src_ref=rsend.at[r, q, :, at], dst_ref=rrecv.at[slot, r, :, at],
+            send_sem=rssem.at[r, i, k], recv_sem=rrsem.at[r, i, slot],
+            device_id={"pair": q}, device_id_type=MESH,
+        )
 
     def reduce_start(r):
-        rsend[r] = acc[r].astype(rsend.dtype)
-        for k in range(n_p - 1):
-            scatter(r, k).start()
+        for i in range(tiles):
+            at = slice(i * tile_n, (i + 1) * tile_n)
+            block = acc[at, :].T.reshape(n_p, h, tile_n)
+            part[r, :, :, at] = block
+            rsend[r, :, :, at] = block.astype(rsend.dtype)
+            for k in range(n_p - 1):
+                scatter(r, i, k, q_of[k], p).start()
 
     def reduce_end(r):
-        total = acc[r, p]
-        for q in q_of:
-            scatter_wait(r, q)
-            total = total + rrecv[q, r].astype(jnp.float32)
-        cyc_out[r * h:(r + 1) * h, :] = total
+        for i in range(tiles):
+            at = slice(i * tile_n, (i + 1) * tile_n)
+            total = part[r, p, :, at]
+            for q in q_of:
+                scatter(r, i, 0, q, q).wait_recv()
+                total = total + rrecv[q, r, :, at].astype(jnp.float32)
+            low = cden[r * h:(r + 1) * h, :] + rden[:, at]
+            cyc_out[r * h:(r + 1) * h, at] = (total / low).astype(cyc_out.dtype)
+
+    def iota(shape, dim):
+        return lax.broadcasted_iota(jnp.int32, shape, dim)
+
+    def pick(hits, values, axis):
+        return jnp.sum(jnp.where(hits, values, jnp.zeros_like(values)), axis=axis, keepdims=True)
+
+    def denominators():
+        n_o, n_v = occ.shape[1], vir.shape[1]
+        occ_row, vir_row = occ[...], vir[...]
+        want = pick(iota((W, n_v), 0) == iota((W, n_v), 1), wlist[...], 1)
+        ewin_col = pick(iota((W, n_v), 1) == want, vir_row, 1)
+        ewin_row = pick(iota((W, W), 0) == iota((W, W), 1), ewin_col, 0)
+        occ_col = pick(iota((n_o, n_o), 0) == iota((n_o, n_o), 1), occ_row, 1)
+        line = p * rows + iota((rows, n_o), 0)
+        occ_j = pick(iota((rows, n_o), 1) == lax.div(line, W), occ_row, 1)
+        ewin_b = pick(iota((rows, W), 1) == lax.rem(iota((rows, W), 0), W), ewin_row, 1)
+        cden[...] = occ_j - ewin_b
+        for i in range(cols // n_v):
+            at = g * (cols // n_v) + i
+            rden[:, i * n_v:(i + 1) * n_v] = pick(iota((1, n_o), 1) == at, occ_row, 1) - vir_row
+        pair = plist[...]
+        o_i = pick(iota((n_o, n_pairs), 0) == lax.div(pair, n_o), occ_col, 0)
+        o_j = pick(iota((n_o, n_pairs), 0) == lax.rem(pair, n_o), occ_col, 0)
+        ab = iota((W * W, W), 0)
+        e_a = pick(iota((W * W, W), 1) == lax.div(ab, W), ewin_row, 1)
+        e_b = pick(iota((W * W, W), 1) == lax.rem(ab, W), ewin_row, 1)
+        lden[...] = (o_i + o_j) - (e_a + e_b)
 
     def spread(buf, slot, send, recv, k):
         q = q_of[k]
@@ -231,11 +262,9 @@
         total = lbuf[0]
         for s in range(1, n_g):
             total = total + lbuf[s]
-        lad_out[...] = total
-
-    def chunk(r, extra):
-        if r + 1 < CHUNKS:
-            own_send(r + 1, begin)
+        lad_out[...] = total / lden[...]
+
+    def chunk(r, before, extra):
         product(r, g, first=True)
         if r == 0:
             spread_wait(xbuf, xsend, xrecv)
@@ -244,13 +273,17 @@
             own_send(item_y, begin)
         hop(r, sib, 1, sib).wait_recv()
         product(r, sib)
+        before()
 
         def step(t, carry):
             forward(r, t, True, begin)
             if r == 0:
                 forward(item_y, t, True, begin)
-            if extra is not None:
-                extra(t)
+            if r + 1 < CHUNKS:
+                @pl.when(t == 1)
+                def _():
+                    own_send(r + 1, begin)
+            extra(t)
 
             def use(d, sz):
                 product(r, sz * 2 + c)
@@ -268,7 +301,7 @@
     spread_all(xbuf, xsend, xrecv)
     load_a.wait()
     own_send(0, begin)
-    chunk(0, None)
+    chunk(0, denominators, lambda t: None)
     hop(item_y, sib, 1, sib).wait_recv()
 
     def rest(t, carry):
@@ -278,22 +311,31 @@
     lax.fori_loop(1, n_z, rest, 0)
     tile_part()
     spread_all(zbuf, zsend, zrecv)
-    chunk(1, None)
-    reduce_end(0)
-    spread_wait(zbuf, zsend, zrecv)
-    weights()
-    load_t.wait()
-    for r in range(2, CHUNKS):
-        if r == 2:
-            chunk(r, ladder_piece)
-            ladder_piece(0)
+
+    def ladder_begin():
+        spread_wait(zbuf, zsend, zrecv)
+        weights()
+        load_t.wait()
+        ladder_piece(0)
+        ladder_piece(n_z - 1)
+
+    def ladder_next(t):
+        @pl.when(t < n_z - 1)
+        def _():
+            ladder_piece(t)
+
+        @pl.when(t == n_z - 1)
+        def _():
             ladder_send()
-        else:
-            chunk(r, None)
-        if r + 1 < CHUNKS:
-            reduce_end(r - 1)
+
+    for r in range(1, CHUNKS):
+        chunk(
+            r,
+            ladder_begin if r == 1 else (lambda: None),
+            ladder_next if r == 1 else (lambda t: None),
+        )
+        reduce_end(r - 1)
     ladder_end()
-    reduce_end(CHUNKS - 2)
     reduce_end(CHUNKS - 1)
 
     def sent(cp):
@@ -311,18 +353,24 @@
         spread(xbuf, p, xsend, xrecv, k).wait_send()
         spread(zbuf, p, zsend, zrecv, k).wait_send()
         for r in range(CHUNKS):
-            scatter(r, k).wait_send()
+            for i in range(tiles):
+                scatter(r, i, k, q_of[k], p).wait_send()
     for k in range(n_g - 1):
         lad_copy(k, g).wait_send()
 
 
-def fused(n_p, n_g, amplitudes, cycle_matrix, fit_panel, pair_amps):
+def tile_of(cols):
+    return 1024 if cols % 1024 == 0 else cols
+
+
+def fused(n_p, n_g, amplitudes, cycle_matrix, fit_panel, pair_amps, *small):
     rows = amplitudes.shape[0] // n_p
     depth = amplitudes.shape[1]
     cols = cycle_matrix.shape[0]
     n_pairs, own_c, n_v = pair_amps.shape
     aux = fit_panel.shape[2]
     h = rows // CHUNKS
+    tiles = cols // tile_of(cols)
     bf, f32 = jnp.bfloat16, jnp.float32
     dma = pltpu.SemaphoreType.DMA
     hbm = pl.BlockSpec(memory_space=pl.ANY)
@@ -330,10 +378,10 @@
     return pl.pallas_call(
         functools.partial(kernel, n_p, n_g),
         out_shape=(
-            jax.ShapeDtypeStruct((rows, cols), f32),
+            jax.ShapeDtypeStruct((rows, cols), bf),
             jax.ShapeDtypeStruct((W * W, n_pairs), f32),
         ),
-        in_specs=[hbm] * 4,
+        in_specs=[hbm] * 4 + [vmem] * 4,
         out_specs=(vmem, vmem),
         scratch_shapes=[
             pltpu.VMEM((n_g, n_p, rows, depth), bf),
@@ -345,9 +393,13 @@
             pltpu.VMEM((own_c // SUB, W * W * SUB, n_v), bf),
             pltpu.VMEM((n_pairs, W * W * SUB), f32),
             pltpu.VMEM((n_g, W * W, n_pairs), f32),
+            pltpu.VMEM((cols, n_p * h), f32),
             pltpu.VMEM((CHUNKS, n_p, h, cols), f32),
             pltpu.VMEM((CHUNKS, n_p, h, cols), bf),
             pltpu.VMEM((n_p, CHUNKS, h, cols), bf),
+            pltpu.VMEM((rows, 1), f32),
+            pltpu.VMEM((1, cols), f32),
+            pltpu.VMEM((W * W, n_pairs), f32),
             dma((n_g,)),
             dma((3,)),
             dma((CHUNKS + 1, n_g)),
@@ -356,8 +408,8 @@
             dma((n_p,)),
             dma((n_p,)),
             dma((n_p,)),
-            dma((CHUNKS, n_p)),
-            dma((CHUNKS, n_p)),
+            dma((CHUNKS, tiles, n_p)),
+            dma((CHUNKS, tiles, n_p)),
             dma((n_g,)),
             dma((n_g,)),
         ],
@@ -369,10 +421,11 @@
         cycle_matrix,
         fit_panel.reshape(W * own_c, aux),
         pair_amps,
+        *[x.reshape(1, x.shape[0]) for x in small],
     )
 
 
-def plain(n_p, n_g, amplitudes, cycle_matrix, fit_panel, pair_amps):
+def plain(amplitudes, cycle_matrix, fit_panel, pair_amps):
     partial_cycle = lax.dot_general(
         lax.all_gather(amplitudes, "grid", axis=1, tiled=True),
         cycle_matrix,
@@ -392,15 +445,17 @@
     partial_ladder = lax.dot_general(
         flat_amps, flat_tile, NT, preferred_element_type=jnp.float32
     )
-    return cycle_sum, lax.psum(partial_ladder, "grid").T
-
-
-def suits(n_p, n_g, amplitudes, fit_panel, pair_amps):
+    return cycle_sum, lax.psum(partial_ladder, "grid")
+
+
+def suits(n_p, n_g, amplitudes, cycle_matrix, fit_panel, pair_amps):
     rows = amplitudes.shape[0] // n_p
     return (
         n_p == W
         and n_g % 2 == 0
         and rows % (CHUNKS * SUB) == 0
+        and n_p * rows % (CHUNKS * 128) == 0
+        and cycle_matrix.shape[0] % pair_amps.shape[2] == 0
         and amplitudes.shape[1] % 128 == 0
         and fit_panel.shape[2] % 128 == 0
         and pair_amps.shape[1] % SUB == 0
@@ -413,10 +468,15 @@
     n_p, n_g,
     cycle_matrix, amplitudes, fit_panel, pair_amps, pair_list, window_list, occ_energy, vir_energy
 ):
+    arrays = (amplitudes, cycle_matrix, fit_panel, pair_amps)
+    if suits(n_p, n_g, *arrays):
+        cycle_update, ladder = fused(
+            n_p, n_g, *arrays, pair_list, window_list, occ_energy, vir_energy
+        )
+        return cycle_update, ladder.T
     window_energy = lookup(vir_energy, window_list[:W])
     local_rows = cycle_matrix.shape[0]
-    form = fused if suits(n_p, n_g, amplitudes, fit_panel, pair_amps) else plain
-    cycle_sum, ladder = form(n_p, n_g, amplitudes, cycle_matrix, fit_panel, pair_amps)
+    cycle_sum, ladder = plain(*arrays)
     column_ids = lax.axis_index("pair") * cycle_sum.shape[0] + jnp.arange(
         cycle_sum.shape[0], dtype=jnp.int32
     )
@@ -426,7 +486,7 @@
     cycle_update = (cycle_sum / (col_energy[:, None] + row_energy[None, :])).astype(jnp.bfloat16)
     pair_energy = lookup(occ_energy, pair_list // O) + lookup(occ_energy, pair_list % O)
     win_pair = (window_energy[:, None] + window_energy[None, :]).reshape(W * W)
-    ladder_update = ladder.T / (pair_energy[:, None] - win_pair[None, :])
+    ladder_update = ladder / (pair_energy[:, None] - win_pair[None, :])
     return (cycle_update, ladder_update)
 
 

time: 121 us -> 95.8 us (0.79)
  Pallas kernels: 110 us -> 89.3 us
  other arithmetic: 9.02 us -> 0 us
  local copies, waits for them, and re-layouts: 0.78 us -> 5.58 us
    pallas_call x1, Pallas kernels: 110 us -> 89.3 us  [fused(): pl.pallas_call(functools.partial(kernel, n_p, n_g), out_shape=(jax.ShapeD...]
    reduce_sum x6 -> x0, other arithmetic: 5.44 us -> none  [lookup(): return jnp.sum(jnp.where(hits, table[None, :], jnp.float32(0.0)), axis=1)]
    unnamed x4 -> x2, local copies, waits for them, and re-layouts: 0.01 us -> 3.09 us
    reshape x0 -> x2, local copies, waits for them, and re-layouts: none -> 2.49 us  [fused(): x.reshape(1, x.shape[0])]
    convert_element_type x1 -> x0, other arithmetic: 2.06 us -> none  [local(): (cycle_sum / (col_energy[:, None] + row_energy[None, :])).astype(jnp.bflo...]
    div x1 -> x0, other arithmetic: 1.4 us -> none  [local(): ladder_update = ladder.T / (pair_energy[:, None] - win_pair[None, :])]
where the time goes in v2:
time: 95.8 us; the launch traced here: 95.5 us
  Pallas kernels  89.3 us (93%)
  local copies, waits for them, and re-layouts  5.58 us (6%)
    pallas_call x1, Pallas kernels, fused(): pl.pallas_call(functools.partial(kernel, n_p, n_g), out_shape=(jax.ShapeD...  89.3 us
    unnamed x2, local copies, waits for them, and re-layouts  3.09 us
    reshape x2, local copies, waits for them, and re-layouts, fused(): x.reshape(1, x.shape[0])  2.49 us

profile of v2, /device:TPU:0, one launch (start us, length us, event | category | flops | bytes accessed | tf_op | source)
XLA Modules:
  0.0 95.5 jit_solution(7047625992757372237)
XLA Ops:
  0.6 1.2 %reshape.25.wlist = s32[1,384]{1,0:T(1,128)} reshape(s32[384]{0:T(512)} %param.13) | data formatting | bytes 3072 | tf_op jit(solution)/shard_map/reshape | solution.py:424
  1.9 1.2 %reshape.27.vir = f32[1,384]{1,0:T(1,128)} reshape(f32[384]{0:T(512)} %param.15) | data formatting | bytes 3072 | tf_op jit(solution)/shard_map/reshape | solution.py:424
  3.1 89.3 %shard_map.95 = (bf16[64,3072]{1,0:T(8,128)(2,1)}, f32[16,256]{1,0:T(8,128)}) custom-call(bf16[4,64,768]{2,1,0:T(8,128)(2,1)} %bitcast.5, bf16[3072,6144]{1,0:T(8,128)(2,1)} %mat.1, bf16[192,256]{1,0:T(8,128)(2,1)} %bitcast.6, bf16[256,48,384]{2,1,0:T(8,128)(2,1)} %pairs.1, s32[1,256]{1,0:T(1,128)} %bitcast.8, s32[1,384]{1,0:T(1,128)} %reshape.25.wlist, ...), custom_call_target="tpu_custom_call" | custom-call | tf_op jit(solution)/shard_map/pallas_call | solution.py:378
  92.4 1.8 %copy.12 = bf16[64,3072]{1,0:T(8,128)(2,1)} copy(bf16[64,3072]{1,0:T(8,128)(2,1)} %get-tuple-element.8) | data formatting | bytes 786432
  94.2 1.3 %copy.13 = f32[256,16]{0,1:T(8,128)} copy(f32[256,16]{0,1:T(8,128)} %bitcast.7) | data formatting | bytes 32768

commit v3 on v2

--- a/solution.py
+++ b/solution.py
@@ -59,16 +59,17 @@
 
     load_m(g).start()
     load_m(sib).start()
-    for t in range(1, n_z):
-        for d in (1, -1):
-            sz = z - d * t
-
-            @pl.when(jnp.logical_and(sz >= 0, sz < n_z))
-            def _():
-                load_m(sz * 2 + c).start()
-                load_m(sz * 2 + 1 - c).start()
     load_t = pltpu.make_async_copy(pairs, tbuf, lsem.at[2])
-    load_t.start()
+
+    def load_far(ts):
+        for t in ts:
+            for d in (1, -1):
+                sz = z - d * t
+
+                @pl.when(jnp.logical_and(sz >= 0, sz < n_z))
+                def _(sz=sz):
+                    load_m(sz * 2 + c).start()
+                    load_m(sz * 2 + 1 - c).start()
 
     barrier = pltpu.get_barrier_semaphore()
     for q in q_of:
@@ -89,23 +90,25 @@
             device_id={"grid": target}, device_id_type=MESH,
         )
 
+    reach = max(1, n_z // 2)
+    near, far = range(1, reach + 1), range(reach + 1, n_z)
+
     def own_send(item, act):
-        @pl.when(z + 1 < n_z)
-        def _():
-            act(hop(item, g, 0, g + 2))
-
-        @pl.when(z >= 1)
-        def _():
-            act(hop(item, g, 2, g - 2))
-
-        act(hop(item, g, 1, sib))
+        act(hop(item, g, 0, sib))
+        for t in near:
+            for j, d in enumerate((1, -1)):
+                to = z + d * t
+
+                @pl.when(jnp.logical_and(to >= 0, to < n_z))
+                def _(t=t, j=j, to=to):
+                    act(hop(item, g, 2 + j * reach + t - 1, to * 2 + c))
 
     def each_line(t, body):
         for d in (1, -1):
             sz = z - d * t
 
             @pl.when(jnp.logical_and(sz >= 0, sz < n_z))
-            def _():
+            def _(d=d, sz=sz):
                 body(d, sz)
 
     def forward(item, t, wait_first, act):
@@ -113,31 +116,35 @@
             s = sz * 2 + c
             if wait_first:
                 hop(item, s, 0, sib).wait_recv()
-            nz = z + d
-
-            @pl.when(jnp.logical_and(nz >= 0, nz < n_z))
-            def _():
-                act(hop(item, s, 0, nz * 2 + c))
-
-            act(hop(item, s, 1, sib))
+            if t >= reach:
+                nz = z + d
+
+                @pl.when(jnp.logical_and(nz >= 0, nz < n_z))
+                def _():
+                    act(hop(item, s, 1, nz * 2 + c))
+
+            act(hop(item, s, 0, sib))
 
         each_line(t, body)
 
     def begin(cp):
         cp.start()
+
+    def product_tile(r, s, i, first=False):
+        at = pl.ds(i * tile_n if isinstance(i, int) else pl.multiple_of(i * tile_n, 128), tile_n)
+        rhs = abuf[s, :, r * h:(r + 1) * h, :].reshape(n_p * h, depth)
+        out = dot_nt(mbuf[s, at, :], rhs)
+        if first:
+            acc[at, :] = out
+        else:
+            acc[at, :] += out
 
     def product(r, s, first=False):
         if r == 0:
             load_m(s).wait()
 
         def tile(i, carry):
-            at = pl.ds(pl.multiple_of(i * tile_n, 128), tile_n)
-            rhs = abuf[s, :, r * h:(r + 1) * h, :].reshape(n_p * h, depth)
-            out = dot_nt(mbuf[s, at, :], rhs)
-            if first:
-                acc[at, :] = out
-            else:
-                acc[at, :] += out
+            product_tile(r, s, i, first)
             return carry
 
         lax.fori_loop(0, tiles, tile, 0)
@@ -150,8 +157,9 @@
             device_id={"pair": q}, device_id_type=MESH,
         )
 
-    def reduce_start(r):
+    def reduce_start(r, last):
         for i in range(tiles):
+            last(i)
             at = slice(i * tile_n, (i + 1) * tile_n)
             block = acc[at, :].T.reshape(n_p, h, tile_n)
             part[r, :, :, at] = block
@@ -264,77 +272,91 @@
             total = total + lbuf[s]
         lad_out[...] = total / lden[...]
 
-    def chunk(r, before, extra):
-        product(r, g, first=True)
-        if r == 0:
-            spread_wait(xbuf, xsend, xrecv)
-            mine = pl.ds(pl.multiple_of(p * own_c, SUB), own_c)
-            ybuf[:, g] = xbuf[:, mine, :]
-            own_send(item_y, begin)
-        hop(r, sib, 1, sib).wait_recv()
-        product(r, sib)
-        before()
-
-        def step(t, carry):
-            forward(r, t, True, begin)
+    def use(r, t):
+        def body(d, sz):
+            product(r, sz * 2 + c)
+            s = sz * 2 + 1 - c
+            hop(r, s, 0, sib).wait_recv()
+            product(r, s)
+
+        each_line(t, body)
+
+    def use_last(r):
+        if len(far) == 0:
+            return lambda i: None
+        t = far[-1]
+
+        def arrive(d, sz):
+            s = sz * 2 + 1 - c
+            hop(r, s, 0, sib).wait_recv()
             if r == 0:
-                forward(item_y, t, True, begin)
-            if r + 1 < CHUNKS:
-                @pl.when(t == 1)
-                def _():
-                    own_send(r + 1, begin)
-            extra(t)
-
-            def use(d, sz):
-                product(r, sz * 2 + c)
-                s = sz * 2 + 1 - c
-                hop(r, s, 1, sib).wait_recv()
-                product(r, s)
-
-            each_line(t, use)
-            return carry
-
-        lax.fori_loop(1, n_z, step, 0)
-        reduce_start(r)
+                load_m(s).wait()
+                load_m(sz * 2 + c).wait()
+
+        each_line(t, arrive)
+
+        def last(i):
+            def body(d, sz):
+                product_tile(r, sz * 2 + c, i)
+                product_tile(r, sz * 2 + 1 - c, i)
+
+            each_line(t, body)
+
+        return last
 
     load_x.wait()
     spread_all(xbuf, xsend, xrecv)
     load_a.wait()
     own_send(0, begin)
-    chunk(0, denominators, lambda t: None)
-    hop(item_y, sib, 1, sib).wait_recv()
-
-    def rest(t, carry):
-        each_line(t, lambda d, sz: hop(item_y, sz * 2 + 1 - c, 1, sib).wait_recv())
-        return carry
-
-    lax.fori_loop(1, n_z, rest, 0)
-    tile_part()
-    spread_all(zbuf, zsend, zrecv)
-
-    def ladder_begin():
-        spread_wait(zbuf, zsend, zrecv)
-        weights()
-        load_t.wait()
-        ladder_piece(0)
-        ladder_piece(n_z - 1)
-
-    def ladder_next(t):
-        @pl.when(t < n_z - 1)
-        def _():
-            ladder_piece(t)
-
-        @pl.when(t == n_z - 1)
-        def _():
+    load_far(near[:1])
+    denominators()
+    spread_wait(xbuf, xsend, xrecv)
+    mine = pl.ds(pl.multiple_of(p * own_c, SUB), own_c)
+    ybuf[:, g] = xbuf[:, mine, :]
+    own_send(item_y, begin)
+
+    for r in range(CHUNKS):
+        product(r, g, first=True)
+        if r == 0:
+            load_far(range(2, n_z))
+        for t in near:
+            forward(r, t, True, begin)
+        if r == 0:
+            for t in near:
+                forward(item_y, t, True, begin)
+            load_t.start()
+        if r + 1 < CHUNKS:
+            own_send(r + 1, begin)
+        hop(r, sib, 0, sib).wait_recv()
+        product(r, sib)
+        for t in near:
+            use(r, t)
+        if r == 0:
+            for t in far:
+                forward(item_y, t, True, begin)
+            hop(item_y, sib, 0, sib).wait_recv()
+            for t in range(1, n_z):
+                each_line(t, lambda d, sz: hop(item_y, sz * 2 + 1 - c, 0, sib).wait_recv())
+            tile_part()
+            spread_all(zbuf, zsend, zrecv)
+        if r == 1:
+            spread_wait(zbuf, zsend, zrecv)
+            weights()
+            load_t.wait()
+
+            def pieces(i, carry):
+                ladder_piece(i)
+                return carry
+
+            lax.fori_loop(0, n_z, pieces, 0)
             ladder_send()
-
-    for r in range(1, CHUNKS):
-        chunk(
-            r,
-            ladder_begin if r == 1 else (lambda: None),
-            ladder_next if r == 1 else (lambda t: None),
-        )
-        reduce_end(r - 1)
+        for t in far:
+            forward(r, t, True, begin)
+            if t != far[-1]:
+                use(r, t)
+        reduce_start(r, use_last(r))
+        if r >= 1:
+            reduce_end(r - 1)
     ladder_end()
     reduce_end(CHUNKS - 1)
 
@@ -343,12 +365,8 @@
 
     for item in range(CHUNKS + 1):
         own_send(item, sent)
-
-        def step(t, carry, item=item):
+        for t in range(1, n_z):
             forward(item, t, False, sent)
-            return carry
-
-        lax.fori_loop(1, n_z, step, 0)
     for k in range(n_p - 1):
         spread(xbuf, p, xsend, xrecv, k).wait_send()
         spread(zbuf, p, zsend, zrecv, k).wait_send()
@@ -403,7 +421,7 @@
             dma((n_g,)),
             dma((3,)),
             dma((CHUNKS + 1, n_g)),
-            dma((CHUNKS + 1, n_g, 3)),
+            dma((CHUNKS + 1, n_g, 2 + 2 * max(1, n_g // 4))),
             dma((n_p,)),
             dma((n_p,)),
             dma((n_p,)),

time: 95.8 us -> 79.6 us (0.83)
  Pallas kernels: 89.3 us -> 73 us
    pallas_call x1, Pallas kernels: 89.3 us -> 73 us  [fused(): pl.pallas_call(functools.partial(kernel, n_p, n_g), out_shape=(jax.ShapeD...]
where the time goes in v3:
time: 79.6 us; the launch traced here: 79.2 us
  Pallas kernels  73 us (92%)
  local copies, waits for them, and re-layouts  5.58 us (7%)
    pallas_call x1, Pallas kernels, fused(): pl.pallas_call(functools.partial(kernel, n_p, n_g), out_shape=(jax.ShapeD...  73 us
    unnamed x2, local copies, waits for them, and re-layouts  3.09 us
    reshape x2, local copies, waits for them, and re-layouts, fused(): x.reshape(1, x.shape[0])  2.49 us

profile of v3, /device:TPU:0, one launch (start us, length us, event | category | flops | bytes accessed | tf_op | source)
XLA Modules:
  0.0 79.2 jit_solution(13558780107031574941)
XLA Ops:
  0.6 1.2 %reshape.25.wlist = s32[1,384]{1,0:T(1,128)} reshape(s32[384]{0:T(512)} %param.13) | data formatting | bytes 3072 | tf_op jit(solution)/shard_map/reshape | solution.py:442
  1.9 1.2 %reshape.27.vir = f32[1,384]{1,0:T(1,128)} reshape(f32[384]{0:T(512)} %param.15) | data formatting | bytes 3072 | tf_op jit(solution)/shard_map/reshape | solution.py:442
  3.1 73.0 %shard_map.95 = (bf16[64,3072]{1,0:T(8,128)(2,1)}, f32[16,256]{1,0:T(8,128)}) custom-call(bf16[4,64,768]{2,1,0:T(8,128)(2,1)} %bitcast.5, bf16[3072,6144]{1,0:T(8,128)(2,1)} %mat.1, bf16[192,256]{1,0:T(8,128)(2,1)} %bitcast.6, bf16[256,48,384]{2,1,0:T(8,128)(2,1)} %pairs.1, s32[1,256]{1,0:T(1,128)} %bitcast.8, s32[1,384]{1,0:T(1,128)} %reshape.25.wlist, ...), custom_call_target="tpu_custom_call" | custom-call | tf_op jit(solution)/shard_map/pallas_call | solution.py:396
  76.1 1.8 %copy.12 = bf16[64,3072]{1,0:T(8,128)(2,1)} copy(bf16[64,3072]{1,0:T(8,128)(2,1)} %get-tuple-element.8) | data formatting | bytes 786432
  77.9 1.3 %copy.13 = f32[256,16]{0,1:T(8,128)} copy(f32[256,16]{0,1:T(8,128)} %bitcast.7) | data formatting | bytes 32768
